TPU v7x, 256 devices: a whole 4x4x8 slice. The times are simulated.
256 devices in a mesh: gx: 32 (over y, z_hi, core), gy: 8 (over z_lo, x).
Axes of the slice: x: 4, y: 4, z: 8 (z_hi: 4, z_lo: 2; z = z_hi * 2 + z_lo), core: 2. Of those that a mesh axis runs over, the one named last changes fastest.
Arguments:
- level_set: float32 [256, 64, 256], P('gx', 'gy'), may hold values from -6 to 6
- source: float32 [256, 64, 256], P('gx', 'gy'), may hold values from -8 to 8
- stiffness: float32 [256, 64, 256], P('gx', 'gy'), may hold values from 0.1 to 6
- snap_buffer: bfloat16 [8, 64, 16, 64], P(None, 'gx', 'gy'), may hold values from -4 to 4
- buffer_order: int32 [8], replicated, may hold values from 0 to 7, each once
- first_weight: bfloat16 [27, 64], replicated, may hold values from -1.25 to 1.25
- second_weight: bfloat16 [1728, 64], replicated, may hold values from -0.15625 to 0.15625
- out_grad: bfloat16 [8, 64, 16, 4096], P('gy', 'gx'), may hold values from -0.15625 to 0.15625
Outputs:
- new_level: float32 [256, 64, 256], P('gx', 'gy')
- pressure: float32 [256, 64, 256], P('gx', 'gy')
- dw_first: float32 [27, 64], replicated
- dw_second: float32 [1728, 64], replicated
Inputs may be any that keep to these rules, and one draw needn't show every extreme that they name: buffer_order holds every slot of 0 to 7 once.
All inputs are finite; a program needn't handle non-finite values.
Results may differ from a plain program's by a relative error of at most 0.0035.
Values may be sent and summed in bfloat16 or wider, within the bound.
A program may use at most 64 MiB of HBM per device.

v0:
```python
import jax
import jax.numpy as jnp
from jax import lax
from jax.sharding import PartitionSpec as P

COARSEN = 4
ITERS = 20
time_step = 2.0


def padded_2(block, sides, width):
    for axis, dim in sides:
        count = lax.axis_size(axis)
        forward = [(i, i + 1) for i in range(count - 1)]
        backward = [(target, source) for source, target in forward]
        low = lax.ppermute(
            lax.slice_in_dim(block, block.shape[dim] - width, None, axis=dim), axis, forward
        )
        high = lax.ppermute(lax.slice_in_dim(block, 0, width, axis=dim), axis, backward)
        block = jnp.concatenate([low, block, high], axis=dim)
    return block


def neighbours(padded):
    total = padded[2:, 1:-1, 1:-1] + padded[:-2, 1:-1, 1:-1]
    total = total + padded[1:-1, 2:, 1:-1] + padded[1:-1, :-2, 1:-1]
    return total + padded[1:-1, 1:-1, 2:] + padded[1:-1, 1:-1, :-2]


def advance(p_pad, f_pad, level):
    grad_px = 0.5 * (p_pad[2:, 1:-1, 1:-1] - p_pad[:-2, 1:-1, 1:-1])
    grad_py = 0.5 * (p_pad[1:-1, 2:, 1:-1] - p_pad[1:-1, :-2, 1:-1])
    grad_pz = 0.5 * (p_pad[1:-1, 1:-1, 2:] - p_pad[1:-1, 1:-1, :-2])
    grad_fx = 0.5 * (f_pad[2:, 1:-1, 1:-1] - f_pad[:-2, 1:-1, 1:-1])
    grad_fy = 0.5 * (f_pad[1:-1, 2:, 1:-1] - f_pad[1:-1, :-2, 1:-1])
    grad_fz = 0.5 * (f_pad[1:-1, 1:-1, 2:] - f_pad[1:-1, 1:-1, :-2])
    return level + time_step * (grad_px * grad_fx + grad_py * grad_fy + grad_pz * grad_fz)


def tile_faces(field):
    extended = padded_2(field, (("gx", 0), ("gy", 1)), 1)
    return jnp.pad(extended, ((0, 0), (0, 0), (1, 1)))


def level_stack(padded, nx, ny, nz):
    rows = []
    for dx in range(3):
        for dy in range(3):
            for dz in range(3):
                rows.append(padded[:, dx : dx + nx, dy : dy + ny, dz : dz + nz].reshape(-1))
    return jnp.stack(rows, 0)


def first_layer(stack, weight):
    return lax.dot_general(
        stack, weight, (((0,), (0,)), ((), ())), preferred_element_type=jnp.float32
    )


def second_grad(h_pad, g_flat, nx, ny, nz):
    blocks = []
    for dx in range(3):
        for dy in range(3):
            block = jnp.concatenate(
                [h_pad[:, dx : dx + nx, dy : dy + ny, dz : dz + nz, :] for dz in range(3)], axis=-1
            )
            block = block.reshape(-1, block.shape[-1])
            blocks.append(
                lax.dot_general(
                    block, g_flat, (((0,), (0,)), ((), ())), preferred_element_type=jnp.float32
                )
            )
    return jnp.concatenate(blocks, 0)


def back_features(g_pad, weight, nx, ny, nz):
    chans = g_pad.shape[-1]
    total = jnp.zeros((g_pad.shape[0] * nx * ny * nz, chans), jnp.float32)
    for dx in range(3):
        for dy in range(3):
            block = jnp.concatenate(
                [
                    g_pad[:, 2 - dx : 2 - dx + nx, 2 - dy : 2 - dy + ny, 2 - dz : 2 - dz + nz, :]
                    for dz in range(3)
                ],
                axis=-1,
            )
            block = block.reshape(-1, 3 * chans)
            mats = []
            for dz in range(3):
                off = dx * 9 + dy * 3 + dz
                mats.append(weight[off * chans : (off + 1) * chans, :].T)
            total = total + jnp.dot(
                block, jnp.concatenate(mats, 0), preferred_element_type=jnp.float32
            )
    return total


def silu_slope(z):
    sig = jax.nn.sigmoid(z)
    return sig * (1.0 + z * (1.0 - sig))


def pad_sides(field):
    widths = [(0, 0), (0, 0), (1, 1), (1, 1)] + [(0, 0)] * (field.ndim - 4)
    return jnp.pad(field, widths)


def per_device(
    level_set, source, stiffness, snap_buffer, buffer_order, first_weight, second_weight, out_grad
):

    def sweep(i, press):
        return (source + neighbours(tile_faces(press))) / (6.0 + stiffness)

    pressure = lax.fori_loop(0, ITERS, sweep, jnp.zeros_like(source))
    new_level = advance(tile_faces(pressure), tile_faces(level_set), level_set)
    tile_x, tile_y, tile_z = level_set.shape
    coarse = new_level.reshape(
        tile_x // COARSEN, COARSEN, tile_y // COARSEN, COARSEN, tile_z // COARSEN, COARSEN
    )
    coarse = coarse.mean(axis=(1, 3, 5)).astype(jnp.bfloat16)
    chosen = (jnp.arange(snap_buffer.shape[0], dtype=jnp.int32) == buffer_order[0])[
        :, None, None, None
    ]
    updated = jnp.where(chosen, coarse[None], snap_buffer)
    local_snaps = jnp.take(updated, buffer_order, axis=0)
    snaps = lax.all_to_all(local_snaps, "gy", split_axis=0, concat_axis=2, tiled=True)
    held, nx, ny, nz = snaps.shape
    chans = first_weight.shape[1]
    level_ext = padded_2(snaps, (("gx", 1),), 1)
    stack = level_stack(pad_sides(level_ext), nx, ny, nz)
    z_one = first_layer(stack, first_weight)
    h_one = jax.nn.silu(z_one).astype(jnp.bfloat16).reshape(held, nx, ny, nz * chans)
    h_ext = padded_2(h_one, (("gx", 1),), 1)
    h_pad = pad_sides(h_ext.reshape(held, nx + 2, ny, nz, chans))
    grad_ext = padded_2(out_grad, (("gx", 1),), 1)
    g_pad = pad_sides(grad_ext.reshape(held, nx + 2, ny, nz, chans))
    g_flat = out_grad.reshape(-1, chans)
    dw_two = second_grad(h_pad, g_flat, nx, ny, nz)
    dh_one = back_features(g_pad, second_weight, nx, ny, nz)
    dz_one = (dh_one * silu_slope(z_one)).astype(jnp.bfloat16)
    dw_one = jnp.dot(stack, dz_one, preferred_element_type=jnp.float32)
    dw_first, dw_second = lax.psum((dw_one, dw_two), ("gx", "gy"))
    return (new_level, pressure, dw_first, dw_second)


def solution(mesh):
    placed = (
        P("gx", "gy", None),
        P("gx", "gy", None),
        P("gx", "gy", None),
        P(None, "gx", "gy", None),
        P(),
        P(),
        P(),
        P("gy", "gx", None, None),
    )
    return jax.shard_map(
        per_device,
        mesh=mesh,
        in_specs=placed,
        out_specs=(P("gx", "gy", None), P("gx", "gy", None), P(), P()),
        check_vma=False,
    )
```

profile of v0, /device:TPU:6, one launch (start us, length us, event | category | flops | bytes accessed | tf_op | source)
XLA Modules:
  0.0 799.7 jit_solution(17139841607486464167)
XLA Ops:
  11.0 389.8 %while.13 = (s32[]{:T(128)}, f32[8,8,256]{2,1,0:T(8,128)S(1)}, f32[8,8,256]{2,1,0:T(8,128)}, f32[8,8,256]{2,1,0:T(8,128)}, s32[]{:T(128)}, /*index=5*/s32[]{:T(128)}) while((s32[]{:T(128)}, f32[8,8,256]{2,1,0:T(8,128)S(1)}, f32[8,8,256]{2,1,0:T(8,128)}, f32[8,8,256]{2,1,0:T(8,128)}, s32[]{:T(128)}, /*index=5*/s32[]{:T(128)}) %tuple.151), condition=%wide.region_1.2_spmd.clone, body=%wide.region_0.1_spmd.clone.sunk | while | flops 598371 | bytes 1049615 | solution.py:116
  12.5 6.7 collective-permute-start.1
  38.6 6.0 collective-permute-start.3
  48.6 6.2 collective-permute-start.1
  57.6 6.0 collective-permute-start.3
  76.2 6.0 collective-permute-start.3
  94.8 6.0 collective-permute-start.3
  104.8 6.7 collective-permute-start.1
  114.3 6.0 collective-permute-start.3
  124.2 7.2 collective-permute-start.1
  134.1 6.0 collective-permute-start.3
  144.0 7.2 collective-permute-start.1
  154.0 6.0 collective-permute-start.3
  163.9 7.2 collective-permute-start.1
  183.7 7.2 collective-permute-start.1
  203.6 7.2 collective-permute-start.1
  223.5 7.2 collective-permute-start.1
  243.3 7.2 collective-permute-start.1
  263.2 7.2 collective-permute-start.1
  283.0 7.2 collective-permute-start.1
  302.9 7.2 collective-permute-start.1
  322.7 7.2 collective-permute-start.1
  342.6 7.2 collective-permute-start.1
  362.4 7.2 collective-permute-start.1
  382.3 7.2 collective-permute-start.1
  400.8 6.5 collective-permute-start.5
  410.1 9.1 %collective-permute-start.14 = (bf16[1,1,16,4096]{3,2,1,0:T(8,128)(2,1)S(1)}, bf16[1,1,16,4096]{3,2,1,0:T(8,128)(2,1)}, u32[]{:S(2)}, u32[]{:S(2)}) collective-permute-start(bf16[1,1,16,4096]{3,2,1,0:T(8,128)(2,1)S(1)} %get-tuple-element.140), channel_id=1, source_target_pairs={{0,8},{8,16},{16,24},{24,32},{32,40},{40,48},{48,56},{56,64},{64,7... | collective-permute-start | bytes 393224 | tf_op jit(solution)/shard_map/ppermute | solution.py:16
  421.2 6.3 collective-permute-start.11
  441.2 6.2 all-to-all-start
  464.8 11.2 %collective-permute-start.16 = (bf16[1,1,16,4096]{3,2,1,0:T(8,128)(2,1)S(1)}, bf16[1,1,16,4096]{3,2,1,0:T(8,128)(2,1)S(1)}, u32[]{:S(2)}, u32[]{:S(2)}) collective-permute-start(bf16[1,1,16,4096]{3,2,1,0:T(8,128)(2,1)S(1)} %get-tuple-element.138), channel_id=1, source_target_pairs={{0,8},{8,16},{16,24},{24,32},{32,40},{40,48},{48,56},{56,64},{64,7... | collective-permute-start | bytes 393224 | tf_op jit(solution)/shard_map/ppermute | solution.py:16
  516.9 101.4 %psum.14 = f32[27,64]{1,0:T(8,128)} all-reduce(f32[27,64]{1,0:T(8,128)S(1)} %fusion.14), channel_id=1, replica_groups=mesh['gx'=32,'gy'=8] {'gx','gy'}, use_global_device_ids=true, to_apply=%region_3.4 | all-reduce | flops 1728 | bytes 13824 | tf_op jit(solution)/shard_map/psum | solution.py:144
  618.3 172.8 %all-reduce.8.cloned.1.call-done = f32[1728,64]{0,1:T(8,128)} async-done(((f32[1728,64]{0,1:T(8,128)}), f32[1728,64]{0,1:T(8,128)}) %all-reduce.8.cloned.1.call-update) | async-done | bytes 442384 | tf_op jit(solution)/shard_map/psum | solution.py:144
  (471 shorter events, 307.0 us)
Async XLA Ops:
  7.9 402.2 %collective-permute-start.7 = (f32[1,8,256]{2,1,0:T(8,128)S(1)}, f32[1,8,256]{2,1,0:T(8,128)S(1)}, u32[]{:S(2)}, u32[]{:S(2)}) collective-permute-start(f32[1,8,256]{2,1,0:T(8,128)S(1)} %get-tuple-element.176), channel_id=1, source_target_pairs={{0,8},{8,16},{16,24},{24,32},{32,40},{40,48},{48,56},{56,64},{64,7... | collective-permute-start | bytes 24584 | tf_op jit(solution)/shard_map/ppermute | solution.py:16
  9.6 409.6 %collective-permute-start.6 = (f32[1,8,256]{2,1,0:T(8,128)S(1)}, f32[1,8,256]{2,1,0:T(8,128)S(1)}, u32[]{:S(2)}, u32[]{:S(2)}) collective-permute-start(f32[1,8,256]{2,1,0:T(8,128)S(1)} %get-tuple-element.175), channel_id=1, source_target_pairs={{8,0},{16,8},{24,16},{32,24},{40,32},{48,40},{56,48},{64,56},{72,6... | collective-permute-start | bytes 24584 | tf_op jit(solution)/shard_map/ppermute | solution.py:19
  11.0 8.2 %collective-permute-start = (f32[1,8,256]{2,1,0:T(8,128)S(1)}, f32[1,8,256]{2,1,0:T(8,128)S(1)}, u32[]{:S(2)}, u32[]{:S(2)}) collective-permute-start(f32[1,8,256]{2,1,0:T(8,128)S(1)} %get-tuple-element.249), channel_id=1, source_target_pairs={{8,0},{16,8},{24,16},{32,24},{40,32},{48,40},{56,48},{64,56},{72,6... | collective-permute-start | bytes 24584 | tf_op jit(solution)/shard_map/while/body/eval_jaxpr/ppermute | solution.py:19
  103.5 8.0 %collective-permute-start = (f32[1,8,256]{2,1,0:T(8,128)S(1)}, f32[1,8,256]{2,1,0:T(8,128)S(1)}, u32[]{:S(2)}, u32[]{:S(2)}) collective-permute-start(f32[1,8,256]{2,1,0:T(8,128)S(1)} %get-tuple-element.249), channel_id=1, source_target_pairs={{8,0},{16,8},{24,16},{32,24},{40,32},{48,40},{56,48},{64,56},{72,6... | collective-permute-start | bytes 24584 | tf_op jit(solution)/shard_map/while/body/eval_jaxpr/ppermute | solution.py:19
  122.9 8.5 %collective-permute-start = (f32[1,8,256]{2,1,0:T(8,128)S(1)}, f32[1,8,256]{2,1,0:T(8,128)S(1)}, u32[]{:S(2)}, u32[]{:S(2)}) collective-permute-start(f32[1,8,256]{2,1,0:T(8,128)S(1)} %get-tuple-element.249), channel_id=1, source_target_pairs={{8,0},{16,8},{24,16},{32,24},{40,32},{48,40},{56,48},{64,56},{72,6... | collective-permute-start | bytes 24584 | tf_op jit(solution)/shard_map/while/body/eval_jaxpr/ppermute | solution.py:19
  142.7 8.5 %collective-permute-start = (f32[1,8,256]{2,1,0:T(8,128)S(1)}, f32[1,8,256]{2,1,0:T(8,128)S(1)}, u32[]{:S(2)}, u32[]{:S(2)}) collective-permute-start(f32[1,8,256]{2,1,0:T(8,128)S(1)} %get-tuple-element.249), channel_id=1, source_target_pairs={{8,0},{16,8},{24,16},{32,24},{40,32},{48,40},{56,48},{64,56},{72,6... | collective-permute-start | bytes 24584 | tf_op jit(solution)/shard_map/while/body/eval_jaxpr/ppermute | solution.py:19
  144.0 8.0 collective-permute-start.1
  162.6 8.5 %collective-permute-start = (f32[1,8,256]{2,1,0:T(8,128)S(1)}, f32[1,8,256]{2,1,0:T(8,128)S(1)}, u32[]{:S(2)}, u32[]{:S(2)}) collective-permute-start(f32[1,8,256]{2,1,0:T(8,128)S(1)} %get-tuple-element.249), channel_id=1, source_target_pairs={{8,0},{16,8},{24,16},{32,24},{40,32},{48,40},{56,48},{64,56},{72,6... | collective-permute-start | bytes 24584 | tf_op jit(solution)/shard_map/while/body/eval_jaxpr/ppermute | solution.py:19
  182.4 8.5 %collective-permute-start = (f32[1,8,256]{2,1,0:T(8,128)S(1)}, f32[1,8,256]{2,1,0:T(8,128)S(1)}, u32[]{:S(2)}, u32[]{:S(2)}) collective-permute-start(f32[1,8,256]{2,1,0:T(8,128)S(1)} %get-tuple-element.249), channel_id=1, source_target_pairs={{8,0},{16,8},{24,16},{32,24},{40,32},{48,40},{56,48},{64,56},{72,6... | collective-permute-start | bytes 24584 | tf_op jit(solution)/shard_map/while/body/eval_jaxpr/ppermute | solution.py:19
  202.3 8.5 %collective-permute-start = (f32[1,8,256]{2,1,0:T(8,128)S(1)}, f32[1,8,256]{2,1,0:T(8,128)S(1)}, u32[]{:S(2)}, u32[]{:S(2)}) collective-permute-start(f32[1,8,256]{2,1,0:T(8,128)S(1)} %get-tuple-element.249), channel_id=1, source_target_pairs={{8,0},{16,8},{24,16},{32,24},{40,32},{48,40},{56,48},{64,56},{72,6... | collective-permute-start | bytes 24584 | tf_op jit(solution)/shard_map/while/body/eval_jaxpr/ppermute | solution.py:19
  222.2 8.5 %collective-permute-start = (f32[1,8,256]{2,1,0:T(8,128)S(1)}, f32[1,8,256]{2,1,0:T(8,128)S(1)}, u32[]{:S(2)}, u32[]{:S(2)}) collective-permute-start(f32[1,8,256]{2,1,0:T(8,128)S(1)} %get-tuple-element.249), channel_id=1, source_target_pairs={{8,0},{16,8},{24,16},{32,24},{40,32},{48,40},{56,48},{64,56},{72,6... | collective-permute-start | bytes 24584 | tf_op jit(solution)/shard_map/while/body/eval_jaxpr/ppermute | solution.py:19
  242.0 8.5 %collective-permute-start = (f32[1,8,256]{2,1,0:T(8,128)S(1)}, f32[1,8,256]{2,1,0:T(8,128)S(1)}, u32[]{:S(2)}, u32[]{:S(2)}) collective-permute-start(f32[1,8,256]{2,1,0:T(8,128)S(1)} %get-tuple-element.249), channel_id=1, source_target_pairs={{8,0},{16,8},{24,16},{32,24},{40,32},{48,40},{56,48},{64,56},{72,6... | collective-permute-start | bytes 24584 | tf_op jit(solution)/shard_map/while/body/eval_jaxpr/ppermute | solution.py:19
  261.9 8.5 %collective-permute-start = (f32[1,8,256]{2,1,0:T(8,128)S(1)}, f32[1,8,256]{2,1,0:T(8,128)S(1)}, u32[]{:S(2)}, u32[]{:S(2)}) collective-permute-start(f32[1,8,256]{2,1,0:T(8,128)S(1)} %get-tuple-element.249), channel_id=1, source_target_pairs={{8,0},{16,8},{24,16},{32,24},{40,32},{48,40},{56,48},{64,56},{72,6... | collective-permute-start | bytes 24584 | tf_op jit(solution)/shard_map/while/body/eval_jaxpr/ppermute | solution.py:19
  263.2 8.0 collective-permute-start.1
  281.7 8.5 %collective-permute-start = (f32[1,8,256]{2,1,0:T(8,128)S(1)}, f32[1,8,256]{2,1,0:T(8,128)S(1)}, u32[]{:S(2)}, u32[]{:S(2)}) collective-permute-start(f32[1,8,256]{2,1,0:T(8,128)S(1)} %get-tuple-element.249), channel_id=1, source_target_pairs={{8,0},{16,8},{24,16},{32,24},{40,32},{48,40},{56,48},{64,56},{72,6... | collective-permute-start | bytes 24584 | tf_op jit(solution)/shard_map/while/body/eval_jaxpr/ppermute | solution.py:19
  283.0 8.0 collective-permute-start.1
  301.6 8.5 %collective-permute-start = (f32[1,8,256]{2,1,0:T(8,128)S(1)}, f32[1,8,256]{2,1,0:T(8,128)S(1)}, u32[]{:S(2)}, u32[]{:S(2)}) collective-permute-start(f32[1,8,256]{2,1,0:T(8,128)S(1)} %get-tuple-element.249), channel_id=1, source_target_pairs={{8,0},{16,8},{24,16},{32,24},{40,32},{48,40},{56,48},{64,56},{72,6... | collective-permute-start | bytes 24584 | tf_op jit(solution)/shard_map/while/body/eval_jaxpr/ppermute | solution.py:19
  321.4 8.5 %collective-permute-start = (f32[1,8,256]{2,1,0:T(8,128)S(1)}, f32[1,8,256]{2,1,0:T(8,128)S(1)}, u32[]{:S(2)}, u32[]{:S(2)}) collective-permute-start(f32[1,8,256]{2,1,0:T(8,128)S(1)} %get-tuple-element.249), channel_id=1, source_target_pairs={{8,0},{16,8},{24,16},{32,24},{40,32},{48,40},{56,48},{64,56},{72,6... | collective-permute-start | bytes 24584 | tf_op jit(solution)/shard_map/while/body/eval_jaxpr/ppermute | solution.py:19
  341.3 8.5 %collective-permute-start = (f32[1,8,256]{2,1,0:T(8,128)S(1)}, f32[1,8,256]{2,1,0:T(8,128)S(1)}, u32[]{:S(2)}, u32[]{:S(2)}) collective-permute-start(f32[1,8,256]{2,1,0:T(8,128)S(1)} %get-tuple-element.249), channel_id=1, source_target_pairs={{8,0},{16,8},{24,16},{32,24},{40,32},{48,40},{56,48},{64,56},{72,6... | collective-permute-start | bytes 24584 | tf_op jit(solution)/shard_map/while/body/eval_jaxpr/ppermute | solution.py:19
  361.1 8.5 %collective-permute-start = (f32[1,8,256]{2,1,0:T(8,128)S(1)}, f32[1,8,256]{2,1,0:T(8,128)S(1)}, u32[]{:S(2)}, u32[]{:S(2)}) collective-permute-start(f32[1,8,256]{2,1,0:T(8,128)S(1)} %get-tuple-element.249), channel_id=1, source_target_pairs={{8,0},{16,8},{24,16},{32,24},{40,32},{48,40},{56,48},{64,56},{72,6... | collective-permute-start | bytes 24584 | tf_op jit(solution)/shard_map/while/body/eval_jaxpr/ppermute | solution.py:19
  381.0 8.5 %collective-permute-start = (f32[1,8,256]{2,1,0:T(8,128)S(1)}, f32[1,8,256]{2,1,0:T(8,128)S(1)}, u32[]{:S(2)}, u32[]{:S(2)}) collective-permute-start(f32[1,8,256]{2,1,0:T(8,128)S(1)} %get-tuple-element.249), channel_id=1, source_target_pairs={{8,0},{16,8},{24,16},{32,24},{40,32},{48,40},{56,48},{64,56},{72,6... | collective-permute-start | bytes 24584 | tf_op jit(solution)/shard_map/while/body/eval_jaxpr/ppermute | solution.py:19
  400.8 20.3 %collective-permute-start.5 = (f32[1,8,256]{2,1,0:T(8,128)S(1)}, f32[1,8,256]{2,1,0:T(8,128)S(1)}, u32[]{:S(2)}, u32[]{:S(2)}) collective-permute-start(f32[1,8,256]{2,1,0:T(8,128)S(1)} %get-tuple-element.174), channel_id=1, source_target_pairs={{0,8},{8,16},{16,24},{24,32},{32,40},{40,48},{48,56},{56,64},{64,7... | collective-permute-start | bytes 24584 | tf_op jit(solution)/shard_map/ppermute | solution.py:16
  407.4 20.1 %collective-permute-start.4 = (f32[1,8,256]{2,1,0:T(8,128)S(1)}, f32[1,8,256]{2,1,0:T(8,128)S(1)}, u32[]{:S(2)}, u32[]{:S(2)}) collective-permute-start(f32[1,8,256]{2,1,0:T(8,128)S(1)} %get-tuple-element.173), channel_id=1, source_target_pairs={{8,0},{16,8},{24,16},{32,24},{40,32},{48,40},{56,48},{64,56},{72,6... | collective-permute-start | bytes 24584 | tf_op jit(solution)/shard_map/ppermute | solution.py:19
  408.7 67.3 %collective-permute-start.15 = (bf16[1,1,16,4096]{3,2,1,0:T(8,128)(2,1)S(1)}, bf16[1,1,16,4096]{3,2,1,0:T(8,128)(2,1)}, u32[]{:S(2)}, u32[]{:S(2)}) collective-permute-start(bf16[1,1,16,4096]{3,2,1,0:T(8,128)(2,1)S(1)} %get-tuple-element.141), channel_id=1, source_target_pairs={{8,0},{16,8},{24,16},{32,24},{40,32},{48,40},{56,48},{64,56},{72,6... | collective-permute-start | bytes 393224 | tf_op jit(solution)/shard_map/ppermute | solution.py:19
  410.1 65.9 %collective-permute-start.14 = (bf16[1,1,16,4096]{3,2,1,0:T(8,128)(2,1)S(1)}, bf16[1,1,16,4096]{3,2,1,0:T(8,128)(2,1)}, u32[]{:S(2)}, u32[]{:S(2)}) collective-permute-start(bf16[1,1,16,4096]{3,2,1,0:T(8,128)(2,1)S(1)} %get-tuple-element.140), channel_id=1, source_target_pairs={{0,8},{8,16},{16,24},{24,32},{32,40},{40,48},{48,56},{56,64},{64,7... | collective-permute-start | bytes 393224 | tf_op jit(solution)/shard_map/ppermute | solution.py:16
  419.2 10.3 %collective-permute-start.10 = (f32[10,1,256]{2,1,0:T(1,128)S(1)}, f32[10,1,256]{2,1,0:T(1,128)S(1)}, u32[]{:S(2)}, u32[]{:S(2)}) collective-permute-start(f32[10,1,256]{2,1,0:T(1,128)S(1)} %get-tuple-element.172), channel_id=1, source_target_pairs={{1,0},{2,1},{3,2},{4,3},{5,4},{6,5},{7,6},{9,8},{10,9},{11,10},{12... | collective-permute-start | bytes 30728 | tf_op jit(solution)/shard_map/ppermute | solution.py:19
  421.2 14.4 %collective-permute-start.11 = (f32[10,1,256]{2,1,0:T(1,128)S(1)}, f32[10,1,256]{2,1,0:T(1,128)S(1)}, u32[]{:S(2)}, u32[]{:S(2)}) collective-permute-start(f32[10,1,256]{2,1,0:T(1,128)S(1)} %get-tuple-element.171), channel_id=1, source_target_pairs={{0,1},{1,2},{2,3},{3,4},{4,5},{5,6},{6,7},{8,9},{9,10},{10,11},{11... | collective-permute-start | bytes 30728 | tf_op jit(solution)/shard_map/ppermute | solution.py:16
  427.6 8.2 %collective-permute-start.8 = (f32[10,1,256]{2,1,0:T(1,128)S(1)}, f32[10,1,256]{2,1,0:T(1,128)S(1)}, u32[]{:S(2)}, u32[]{:S(2)}) collective-permute-start(f32[10,1,256]{2,1,0:T(1,128)S(1)} %get-tuple-element.170), channel_id=1, source_target_pairs={{1,0},{2,1},{3,2},{4,3},{5,4},{6,5},{7,6},{9,8},{10,9},{11,10},{12... | collective-permute-start | bytes 30728 | tf_op jit(solution)/shard_map/ppermute | solution.py:19
  441.2 10.2 %all-to-all-start = ((bf16[8,2,128]{2,1,0:T(2,128)(2,1)}), bf16[8,2,128]{2,1,0:T(2,128)(2,1)S(1)}, u32[]{:S(2)}, u32[]{:S(2)}) async-start(bf16[8,2,128]{2,1,0:T(2,128)(2,1)} %reshape.125), calls=%async_computation | async-start | bytes 8192 | tf_op jit(solution)/shard_map/all_to_all | solution.py:128
  447.4 343.7 %all-reduce.8.cloned.1.call-start = ((), (), s32[]{:S(2)}) async-start(), calls=%async_computation.1 | async-start | bytes 917504 | tf_op jit(solution)/shard_map/psum | solution.py:144
  463.5 31.0 %collective-permute-start.17 = (bf16[1,1,16,4096]{3,2,1,0:T(8,128)(2,1)}, bf16[1,1,16,4096]{3,2,1,0:T(8,128)(2,1)S(1)}, u32[]{:S(2)}, u32[]{:S(2)}) collective-permute-start(bf16[1,1,16,4096]{3,2,1,0:T(8,128)(2,1)} %get-tuple-element.139), channel_id=1, source_target_pairs={{8,0},{16,8},{24,16},{32,24},{40,32},{48,40},{56,48},{64,56},{72,6... | collective-permute-start | bytes 393224 | tf_op jit(solution)/shard_map/ppermute | solution.py:19
  464.8 30.0 %collective-permute-start.16 = (bf16[1,1,16,4096]{3,2,1,0:T(8,128)(2,1)S(1)}, bf16[1,1,16,4096]{3,2,1,0:T(8,128)(2,1)S(1)}, u32[]{:S(2)}, u32[]{:S(2)}) collective-permute-start(bf16[1,1,16,4096]{3,2,1,0:T(8,128)(2,1)S(1)} %get-tuple-element.138), channel_id=1, source_target_pairs={{0,8},{8,16},{16,24},{24,32},{32,40},{40,48},{48,56},{56,64},{64,7... | collective-permute-start | bytes 393224 | tf_op jit(solution)/shard_map/ppermute | solution.py:16
  (114 other events, 2252.8 us)
Sparse Core Ops, SparseCore 0:
  516.0 275.0 all-reduce.7
where the time goes:
time: 804 us; the launch traced here: 800 us
  starting transfers between devices  381 us (47%)
  waiting for transfers between devices  220 us (27%)
  blocking collectives  101 us (13%)
  other arithmetic  38 us (5%)
  local copies, waits for them, and re-layouts  31.3 us (4%)
  between operations  15.1 us (2%)
  matrix products  10.3 us (1%)
    ppermute x47, starting transfers between devices, padded_2(): lax.ppermute(lax.slice_in_dim(block, block.shape[dim] - width, None, axis...  300 us
    psum x1, waiting for transfers between devices, per_device(): dw_first, dw_second = lax.psum((dw_one, dw_two), ('gx', 'gy'))  173 us
    psum x1, blocking collectives, per_device(): dw_first, dw_second = lax.psum((dw_one, dw_two), ('gx', 'gy'))  101 us
    ppermute x47, starting transfers between devices, padded_2(): lax.ppermute(lax.slice_in_dim(block, 0, width, axis=dim), axis, backward)  75.5 us
    ppermute x47, waiting for transfers between devices, padded_2(): lax.ppermute(lax.slice_in_dim(block, block.shape[dim] - width, None, axis...  44.2 us
    div x20, other arithmetic, sweep(): return (source + neighbours(tile_faces(press))) / (6.0 + stiffness)  19.4 us
  transfers between devices with their start and end apart: 96, of which 43 were waited for; matrix products, arithmetic and copies ran while one was open for 7% of the time, Pallas kernels for 0%

commit v1 on v0

--- a/solution.py
+++ b/solution.py
@@ -141,7 +141,7 @@
     dh_one = back_features(g_pad, second_weight, nx, ny, nz)
     dz_one = (dh_one * silu_slope(z_one)).astype(jnp.bfloat16)
     dw_one = jnp.dot(stack, dz_one, preferred_element_type=jnp.float32)
-    dw_first, dw_second = lax.psum((dw_one, dw_two), ("gx", "gy"))
+    dw_first, dw_second = lax.psum(lax.psum((dw_one, dw_two), "gy"), "gx")
     return (new_level, pressure, dw_first, dw_second)
 
 

time: 804 us -> 914 us (1.14)
  blocking collectives: 101 us -> 169 us
  waiting for transfers between devices: 220 us -> 256 us
    psum x1 -> x2, blocking collectives: 101 us -> 169 us  [per_device(): dw_first, dw_second = lax.psum(lax.psum((dw_one, dw_two), 'gy'), 'gx')]
    psum x1 -> x2, waiting for transfers between devices: 173 us -> 208 us  [per_device(): dw_first, dw_second = lax.psum(lax.psum((dw_one, dw_two), 'gy'), 'gx')]
  transfers between devices with their start and end apart: 96 -> 97, of which waited for: 43 -> 44; matrix products, arithmetic and copies ran while one was open for 7% -> 6% of each run, Pallas kernels for 0% -> 0%
where the time goes in v1:
time: 914 us; the launch traced here: 910 us
  starting transfers between devices  381 us (42%)
  waiting for transfers between devices  256 us (28%)
  blocking collectives  169 us (18%)
  other arithmetic  40.7 us (4%)
  local copies, waits for them, and re-layouts  31.4 us (3%)
  between operations  15 us (2%)
  matrix products  14.5 us (2%)
    ppermute x47, starting transfers between devices, padded_2(): lax.ppermute(lax.slice_in_dim(block, block.shape[dim] - width, None, axis...  300 us
    psum x2, waiting for transfers between devices, per_device(): dw_first, dw_second = lax.psum(lax.psum((dw_one, dw_two), 'gy'), 'gx')  208 us
    psum x2, blocking collectives, per_device(): dw_first, dw_second = lax.psum(lax.psum((dw_one, dw_two), 'gy'), 'gx')  169 us
    ppermute x47, starting transfers between devices, padded_2(): lax.ppermute(lax.slice_in_dim(block, 0, width, axis=dim), axis, backward)  75.5 us
    ppermute x47, waiting for transfers between devices, padded_2(): lax.ppermute(lax.slice_in_dim(block, block.shape[dim] - width, None, axis...  44.2 us
    div x20, other arithmetic, sweep(): return (source + neighbours(tile_faces(press))) / (6.0 + stiffness)  19.4 us
  transfers between devices with their start and end apart: 97, of which 44 were waited for; matrix products, arithmetic and copies ran while one was open for 6% of the time, Pallas kernels for 0%

profile of v1, /device:TPU:6, one launch (start us, length us, event | category | flops | bytes accessed | tf_op | source)
XLA Modules:
  0.0 909.9 jit_solution(16251401700949222374)
XLA Ops:
  11.0 389.8 %while.13 = (s32[]{:T(128)}, f32[8,8,256]{2,1,0:T(8,128)S(1)}, f32[8,8,256]{2,1,0:T(8,128)}, f32[8,8,256]{2,1,0:T(8,128)}, s32[]{:T(128)}, /*index=5*/s32[]{:T(128)}) while((s32[]{:T(128)}, f32[8,8,256]{2,1,0:T(8,128)S(1)}, f32[8,8,256]{2,1,0:T(8,128)}, f32[8,8,256]{2,1,0:T(8,128)}, s32[]{:T(128)}, /*index=5*/s32[]{:T(128)}) %tuple.151), condition=%wide.region_1.2_spmd.clone, body=%wide.region_0.1_spmd.clone.sunk | while | flops 598371 | bytes 1049615 | solution.py:116
  12.5 6.7 collective-permute-start.1
  38.6 6.0 collective-permute-start.3
  48.6 6.2 collective-permute-start.1
  57.6 6.0 collective-permute-start.3
  76.2 6.0 collective-permute-start.3
  94.8 6.0 collective-permute-start.3
  104.8 6.7 collective-permute-start.1
  114.3 6.0 collective-permute-start.3
  124.2 7.2 collective-permute-start.1
  144.0 7.2 collective-permute-start.1
  163.9 7.2 collective-permute-start.1
  183.7 7.2 collective-permute-start.1
  203.6 7.2 collective-permute-start.1
  223.5 7.2 collective-permute-start.1
  243.3 7.2 collective-permute-start.1
  263.2 7.2 collective-permute-start.1
  283.0 7.2 collective-permute-start.1
  302.9 7.2 collective-permute-start.1
  322.7 7.2 collective-permute-start.1
  342.6 7.2 collective-permute-start.1
  362.4 7.2 collective-permute-start.1
  382.3 7.2 collective-permute-start.1
  400.8 6.5 collective-permute-start.5
  410.1 9.1 collective-permute-start.14
  421.2 6.3 collective-permute-start.11
  441.2 6.2 all-to-all-start
  464.2 11.1 %collective-permute-start.16 = (bf16[1,1,16,4096]{3,2,1,0:T(8,128)(2,1)S(1)}, bf16[1,1,16,4096]{3,2,1,0:T(8,128)(2,1)S(1)}, u32[]{:S(2)}, u32[]{:S(2)}) collective-permute-start(bf16[1,1,16,4096]{3,2,1,0:T(8,128)(2,1)S(1)} %get-tuple-element.138), channel_id=1, source_target_pairs={{0,8},{8,16},{16,24},{24,32},{32,40},{40,48},{48,56},{56,64},{64,7... | collective-permute-start | bytes 393224 | tf_op jit(solution)/shard_map/ppermute | solution.py:16
  521.8 97.7 %all-reduce.9.cloned.1.call-done = f32[1728,64]{0,1:T(8,128)} async-done(((f32[1728,64]{0,1:T(8,128)}), f32[1728,64]{0,1:T(8,128)}) %all-reduce.9.cloned.1.call-update) | async-done | bytes 442384 | tf_op jit(solution)/shard_map/psum | solution.py:144
  621.7 30.3 %psum.28 = f32[27,64]{1,0:T(8,128)S(1)} all-reduce(f32[27,64]{1,0:T(8,128)S(1)} %fusion.14), channel_id=1, replica_groups=mesh['gx'=32,'gy'=8] {'gy'}, use_global_device_ids=true, to_apply=%region_3.4 | all-reduce | flops 1728 | bytes 13824 | tf_op jit(solution)/shard_map/psum | solution.py:144
  652.0 138.6 %psum.29 = f32[27,64]{1,0:T(8,128)} all-reduce(f32[27,64]{1,0:T(8,128)S(1)} %psum.28), channel_id=1, replica_groups=mesh['gx'=32,'gy'=8] {'gx'}, use_global_device_ids=true, to_apply=%region_4.5 | all-reduce | flops 1728 | bytes 13824 | tf_op jit(solution)/shard_map/psum | solution.py:144
  790.6 110.7 %all-reduce.11.cloned.1.call-done = f32[1728,64]{0,1:T(8,128)} async-done(((f32[1728,64]{0,1:T(8,128)}), f32[1728,64]{0,1:T(8,128)}) %all-reduce.11.cloned.1.call-update) | async-done | bytes 442384 | tf_op jit(solution)/shard_map/psum | solution.py:144
  (459 shorter events, 326.3 us)
Async XLA Ops:
  7.9 402.2 %collective-permute-start.7 = (f32[1,8,256]{2,1,0:T(8,128)S(1)}, f32[1,8,256]{2,1,0:T(8,128)S(1)}, u32[]{:S(2)}, u32[]{:S(2)}) collective-permute-start(f32[1,8,256]{2,1,0:T(8,128)S(1)} %get-tuple-element.176), channel_id=1, source_target_pairs={{0,8},{8,16},{16,24},{24,32},{32,40},{40,48},{48,56},{56,64},{64,7... | collective-permute-start | bytes 24584 | tf_op jit(solution)/shard_map/ppermute | solution.py:16
  9.6 409.6 %collective-permute-start.6 = (f32[1,8,256]{2,1,0:T(8,128)S(1)}, f32[1,8,256]{2,1,0:T(8,128)S(1)}, u32[]{:S(2)}, u32[]{:S(2)}) collective-permute-start(f32[1,8,256]{2,1,0:T(8,128)S(1)} %get-tuple-element.175), channel_id=1, source_target_pairs={{8,0},{16,8},{24,16},{32,24},{40,32},{48,40},{56,48},{64,56},{72,6... | collective-permute-start | bytes 24584 | tf_op jit(solution)/shard_map/ppermute | solution.py:19
  11.0 8.2 collective-permute-start
  103.5 8.0 collective-permute-start
  122.9 8.5 collective-permute-start
  142.7 8.5 collective-permute-start
  144.0 8.0 collective-permute-start.1
  162.6 8.5 collective-permute-start
  182.4 8.5 collective-permute-start
  202.3 8.5 collective-permute-start
  222.2 8.5 collective-permute-start
  242.0 8.5 collective-permute-start
  261.9 8.5 collective-permute-start
  263.2 8.0 collective-permute-start.1
  281.7 8.5 collective-permute-start
  301.6 8.5 collective-permute-start
  321.4 8.5 collective-permute-start
  341.3 8.5 collective-permute-start
  361.1 8.5 collective-permute-start
  381.0 8.5 collective-permute-start
  400.8 20.4 %collective-permute-start.5 = (f32[1,8,256]{2,1,0:T(8,128)S(1)}, f32[1,8,256]{2,1,0:T(8,128)S(1)}, u32[]{:S(2)}, u32[]{:S(2)}) collective-permute-start(f32[1,8,256]{2,1,0:T(8,128)S(1)} %get-tuple-element.174), channel_id=1, source_target_pairs={{0,8},{8,16},{16,24},{24,32},{32,40},{40,48},{48,56},{56,64},{64,7... | collective-permute-start | bytes 24584 | tf_op jit(solution)/shard_map/ppermute | solution.py:16
  407.4 20.2 %collective-permute-start.4 = (f32[1,8,256]{2,1,0:T(8,128)S(1)}, f32[1,8,256]{2,1,0:T(8,128)S(1)}, u32[]{:S(2)}, u32[]{:S(2)}) collective-permute-start(f32[1,8,256]{2,1,0:T(8,128)S(1)} %get-tuple-element.173), channel_id=1, source_target_pairs={{8,0},{16,8},{24,16},{32,24},{40,32},{48,40},{56,48},{64,56},{72,6... | collective-permute-start | bytes 24584 | tf_op jit(solution)/shard_map/ppermute | solution.py:19
  408.7 66.6 %collective-permute-start.15 = (bf16[1,1,16,4096]{3,2,1,0:T(8,128)(2,1)S(1)}, bf16[1,1,16,4096]{3,2,1,0:T(8,128)(2,1)}, u32[]{:S(2)}, u32[]{:S(2)}) collective-permute-start(bf16[1,1,16,4096]{3,2,1,0:T(8,128)(2,1)S(1)} %get-tuple-element.141), channel_id=1, source_target_pairs={{8,0},{16,8},{24,16},{32,24},{40,32},{48,40},{56,48},{64,56},{72,6... | collective-permute-start | bytes 393224 | tf_op jit(solution)/shard_map/ppermute | solution.py:19
  410.1 65.2 %collective-permute-start.14 = (bf16[1,1,16,4096]{3,2,1,0:T(8,128)(2,1)S(1)}, bf16[1,1,16,4096]{3,2,1,0:T(8,128)(2,1)}, u32[]{:S(2)}, u32[]{:S(2)}) collective-permute-start(bf16[1,1,16,4096]{3,2,1,0:T(8,128)(2,1)S(1)} %get-tuple-element.140), channel_id=1, source_target_pairs={{0,8},{8,16},{16,24},{24,32},{32,40},{40,48},{48,56},{56,64},{64,7... | collective-permute-start | bytes 393224 | tf_op jit(solution)/shard_map/ppermute | solution.py:16
  419.3 10.3 %collective-permute-start.10 = (f32[10,1,256]{2,1,0:T(1,128)S(1)}, f32[10,1,256]{2,1,0:T(1,128)S(1)}, u32[]{:S(2)}, u32[]{:S(2)}) collective-permute-start(f32[10,1,256]{2,1,0:T(1,128)S(1)} %get-tuple-element.172), channel_id=1, source_target_pairs={{1,0},{2,1},{3,2},{4,3},{5,4},{6,5},{7,6},{9,8},{10,9},{11,10},{12... | collective-permute-start | bytes 30728 | tf_op jit(solution)/shard_map/ppermute | solution.py:19
  421.2 14.4 %collective-permute-start.11 = (f32[10,1,256]{2,1,0:T(1,128)S(1)}, f32[10,1,256]{2,1,0:T(1,128)S(1)}, u32[]{:S(2)}, u32[]{:S(2)}) collective-permute-start(f32[10,1,256]{2,1,0:T(1,128)S(1)} %get-tuple-element.171), channel_id=1, source_target_pairs={{0,1},{1,2},{2,3},{3,4},{4,5},{5,6},{6,7},{8,9},{9,10},{10,11},{11... | collective-permute-start | bytes 30728 | tf_op jit(solution)/shard_map/ppermute | solution.py:16
  427.6 8.2 collective-permute-start.8
  441.2 10.2 %all-to-all-start = ((bf16[8,2,128]{2,1,0:T(2,128)(2,1)}), bf16[8,2,128]{2,1,0:T(2,128)(2,1)S(1)}, u32[]{:S(2)}, u32[]{:S(2)}) async-start(bf16[8,2,128]{2,1,0:T(2,128)(2,1)} %reshape.125), calls=%async_computation | async-start | bytes 8192 | tf_op jit(solution)/shard_map/all_to_all | solution.py:128
  447.4 172.1 %all-reduce.9.cloned.1.call-start = ((), (), s32[]{:S(2)}) async-start(), calls=%async_computation.1 | async-start | bytes 917504 | tf_op jit(solution)/shard_map/psum | solution.py:144
  462.9 29.0 %collective-permute-start.17 = (bf16[1,1,16,4096]{3,2,1,0:T(8,128)(2,1)S(1)}, bf16[1,1,16,4096]{3,2,1,0:T(8,128)(2,1)S(1)}, u32[]{:S(2)}, u32[]{:S(2)}) collective-permute-start(bf16[1,1,16,4096]{3,2,1,0:T(8,128)(2,1)S(1)} %get-tuple-element.139), channel_id=1, source_target_pairs={{8,0},{16,8},{24,16},{32,24},{40,32},{48,40},{56,48},{64,56},{72,6... | collective-permute-start | bytes 393224 | tf_op jit(solution)/shard_map/ppermute | solution.py:19
  464.2 27.9 %collective-permute-start.16 = (bf16[1,1,16,4096]{3,2,1,0:T(8,128)(2,1)S(1)}, bf16[1,1,16,4096]{3,2,1,0:T(8,128)(2,1)S(1)}, u32[]{:S(2)}, u32[]{:S(2)}) collective-permute-start(bf16[1,1,16,4096]{3,2,1,0:T(8,128)(2,1)S(1)} %get-tuple-element.138), channel_id=1, source_target_pairs={{0,8},{8,16},{16,24},{24,32},{32,40},{40,48},{48,56},{56,64},{64,7... | collective-permute-start | bytes 393224 | tf_op jit(solution)/shard_map/ppermute | solution.py:16
  517.7 383.6 %all-reduce.11.cloned.1.call-start = ((), (), s32[]{:S(2)}) async-start(), calls=%async_computation.2 | async-start | bytes 917504 | tf_op jit(solution)/shard_map/psum | solution.py:144
  (107 other events, 3047.9 us)
Sparse Core Ops, SparseCore 0:
  517.8 101.6 all-reduce.8
  622.3 278.9 all-reduce.10
